TPU v7x, 32 devices: a whole 2x2x4 slice. The times are simulated.
32 devices in a mesh: wide: 8 (over y, x, core), narrow: 4 (over z).
Axes of the slice: x: 2, y: 2, z: 4, core: 2. Of those that a mesh axis runs over, the one named last changes fastest.
Arguments:
- tile_flow_speed: float32 [512, 3, 4096], P(('wide', 'narrow')), may hold values from -3 to 3
- tile_stress_mean: float32 [512, 4096], P(('wide', 'narrow')), may hold values from -3 to 3
- tile_heat_state: float32 [512, 4096], P(('wide', 'narrow')), may hold values from 0 to 1
- tile_drag_coefficient: float32 [512, 4096], P(('wide', 'narrow')), may hold values from 0.5 to 2
- marker_attributes: float32 [8, 262144], P(None, ('wide', 'narrow')), may hold values from -6 to 6
- marker_holding_tile: int32 [262144], P(('wide', 'narrow')), may hold values from 0 to 511, as said below
- marker_voxel_number: int32 [262144], P(('wide', 'narrow')), may hold values from 0 to 4095
- prior_slot_of_tile: int32 [512], P(('wide', 'narrow')), may hold values from 0 to 511, as said below
Outputs:
- velocity: float32 [3, 128, 128, 128], P(None, 'wide', 'narrow')
- pressure: float32 [128, 128, 128], P('wide', 'narrow')
- heat_on_fresh_grid: float32 [128, 128, 128], P('wide', 'narrow')
- bin_mean_attributes: float32 [8, 32, 32, 32], P(None, 'wide', 'narrow')
Inputs may be any that keep to these rules, and one draw needn't show every extreme that they name: prior_slot_of_tile is a permutation: new owner q // 16 holds at place q % 16 the block that old owner prior_slot_of_tile[q] // 16 held at place prior_slot_of_tile[q] % 16. Every old owner sends to every new owner either none or exactly 1 of its blocks. `marker_holding_tile`: the tracer at position t is stored on old owner t // 8192 and lies in one of that owner's blocks. The tracers of one old owner whose blocks go to one new owner number at most 640, and every old owner has exactly 640 for one of its new owners.
All inputs are finite; a program needn't handle non-finite values.
Results may differ from a plain program's by a relative error of at most 0.00013.
Values sent between devices are 32-bit elements; how exact they have to be, the bound alone decides.
A program may use at most 256 MiB of HBM per device.

v0:
```python
import functools

import jax
import jax.numpy as jnp
from jax import lax
from jax.experimental import pallas as pl
from jax.experimental.pallas import tpu as pltpu
from jax.sharding import PartitionSpec as P

BS = 16
LX = 1
LY = 2
LZ = 8
SWEEPS = 3
BINS = 64

MIX_WEIGHTS = (0.3, -0.25, 0.2, -0.15, 0.35, -0.3, 0.25, -0.2)
RELAX_WEIGHT = 0.7
PRESSURE_WEIGHT = 0.3
HEAT_FACTOR = 2.0
DENSITY_FACTOR = 4.0
MESH = pl.DeviceIdType.MESH


def bin_kernel(base_ref, holder_ref, voxel_ref, attr_ref, mean_ref, *, blocks, chunk):
    props, tracers = attr_ref.shape
    total_bins = blocks * BINS
    base = base_ref[0]
    bin_ids = lax.broadcasted_iota(jnp.int32, (total_bins, chunk), 0)

    def step(turn, sums):
        at = pl.ds(pl.multiple_of(turn * chunk, chunk), chunk)
        voxel = voxel_ref[:, at]
        key = (
            (holder_ref[:, at] - base) * BINS
            + (voxel >> 10) * 16
            + ((voxel >> 6) & 3) * 4
            + ((voxel >> 2) & 3)
        )
        table = jnp.where(bin_ids == key, 1.0, 0.0).astype(jnp.bfloat16)
        values = attr_ref[:, at]
        high = values.astype(jnp.bfloat16)
        rest = values - high.astype(jnp.float32)
        middle = rest.astype(jnp.bfloat16)
        low = (rest - middle.astype(jnp.float32)).astype(jnp.bfloat16)
        ones = jnp.ones((props, chunk), jnp.bfloat16)
        rows = jnp.concatenate([high, middle, low, ones], axis=0)
        return sums + lax.dot_general(
            rows, table, (((1,), (1,)), ((), ())), preferred_element_type=jnp.float32
        )

    sums = lax.fori_loop(
        0, tracers // chunk, step, jnp.zeros((4 * props, total_bins), jnp.float32)
    )
    total = sums[:props] + sums[props : 2 * props] + sums[2 * props : 3 * props]
    mean_ref[...] = total / jnp.maximum(sums[3 * props :], 1.0)


def bin_means(base, holder, voxel, attributes, blocks):
    props, tracers = attributes.shape
    chunk = 1024 if tracers % 1024 == 0 else tracers
    vmem = pl.BlockSpec(memory_space=pltpu.VMEM)
    return pl.pallas_call(
        functools.partial(bin_kernel, blocks=blocks, chunk=chunk),
        out_shape=jax.ShapeDtypeStruct((props, blocks * BINS), jnp.float32),
        in_specs=[pl.BlockSpec(memory_space=pltpu.SMEM), vmem, vmem, vmem],
        out_specs=vmem,
        compiler_params=pltpu.CompilerParams(vmem_limit_bytes=32 * 1024 * 1024),
        cost_estimate=pl.CostEstimate(
            flops=2 * 32 * tracers * blocks * BINS, bytes_accessed=40 * tracers, transcendentals=0
        ),
    )(base.reshape(1), holder.reshape(1, tracers), voxel.reshape(1, tracers), attributes)


def swap_groups(x):
    row = lax.broadcasted_iota(jnp.int32, x.shape, 1)
    group = lax.broadcasted_iota(jnp.int32, x.shape, 2) // BS
    for bit in (1, 2, 4):
        row_set = (row & bit) != 0
        group_set = (group & bit) != 0
        from_above = pltpu.roll(pltpu.roll(x, 8 - bit, 1), BS * bit, 2)
        from_below = pltpu.roll(pltpu.roll(x, bit, 1), 8 * BS - BS * bit, 2)
        x = jnp.where(
            row_set == group_set, x, jnp.where(group_set, from_above, from_below)
        )
    return x


def pick_kernel(index_ref, from_ref, to_ref, sems):
    count = to_ref.shape[0]

    def copy_of(i):
        return pltpu.make_async_copy(from_ref.at[index_ref[i]], to_ref.at[i], sems.at[i])

    for i in range(count):
        copy_of(i).start()
    for i in range(count):
        copy_of(i).wait()


def pick(index, array):
    return pl.pallas_call(
        pick_kernel,
        out_shape=jax.ShapeDtypeStruct(index.shape + array.shape[1:], array.dtype),
        in_specs=[
            pl.BlockSpec(memory_space=pltpu.SMEM),
            pl.BlockSpec(memory_space=pl.ANY),
        ],
        out_specs=pl.BlockSpec(memory_space=pl.ANY),
        scratch_shapes=[pltpu.SemaphoreType.DMA(index.shape)],
    )(index, array)


def unpack_kernel(slot_ref, recv_ref, mix_ref, state_ref, heat_ref, held, sems):
    places = LY * LZ
    copies = []
    for r in range(places):
        copies.append(
            pltpu.make_async_copy(
                recv_ref.at[slot_ref[r]], held.at[r // LZ, :, r % LZ, :], sems.at[r]
            )
        )
        copies[-1].start()
    for copy in copies:
        copy.wait()
    spread = (
        lax.broadcasted_iota(jnp.int32, (32, 128), 0)
        == lax.broadcasted_iota(jnp.int32, (32, 128), 1) // 4
    ).astype(jnp.float32)
    wide_mix = jnp.dot(
        mix_ref[...], spread, precision=lax.Precision.HIGHEST, preferred_element_type=jnp.float32
    )
    for y in range(LY):
        rows = slice(y * BS, (y + 1) * BS)
        for field in range(4):
            part = swap_groups(held[y, field * 32 : (field + 1) * 32])
            state_ref[field, :, rows, :] = part.reshape(BS, BS, 128)
        heat = swap_groups(held[y, 128:160]).reshape(BS, BS, 128)
        heat_ref[:, rows, :] = heat
        drag = swap_groups(held[y, 160:192]).reshape(BS, BS, 128)
        for layer in range(4):
            piece = wide_mix[layer * 8 + y * 4 : layer * 8 + y * 4 + 4]
            piece = jnp.concatenate(
                [jnp.broadcast_to(piece[j : j + 1], (4, 128)) for j in range(4)], axis=0
            )
            at = slice(layer * 4, layer * 4 + 4)
            state_ref[4, at, rows, :] = drag[at] * jnp.exp(
                HEAT_FACTOR * (0.5 - heat[at]) + piece[None]
            )


def unpack(slots, received, mixture):
    grid_shape = (BS, LY * BS, LZ * BS)
    vmem = pl.BlockSpec(memory_space=pltpu.VMEM)
    return pl.pallas_call(
        unpack_kernel,
        out_shape=(
            jax.ShapeDtypeStruct((5,) + grid_shape, jnp.float32),
            jax.ShapeDtypeStruct(grid_shape, jnp.float32),
        ),
        in_specs=[
            pl.BlockSpec(memory_space=pltpu.SMEM),
            pl.BlockSpec(memory_space=pl.ANY),
            vmem,
        ],
        out_specs=(vmem, vmem),
        scratch_shapes=[
            pltpu.VMEM((LY, 192, LZ, 128), jnp.float32),
            pltpu.SemaphoreType.DMA((LY * LZ,)),
        ],
        compiler_params=pltpu.CompilerParams(vmem_limit_bytes=32 * 1024 * 1024),
    )(slots, received, mixture)


def sweep_kernel(
    state_ref, heat_ref, velocity_ref, pressure_ref,
    pad_0, pad_1, pad_2, edge_out, edge_in, send_sems, recv_sems,
    *, wide_count, narrow_count,
):
    wide, narrow = lax.axis_index("wide"), lax.axis_index("narrow")
    nx, ny, nz = heat_ref.shape
    exists = (wide > 0, wide < wide_count - 1, narrow > 0, narrow < narrow_count - 1)
    partner = ((wide - 1, narrow), (wide + 1, narrow), (wide, narrow - 1), (wide, narrow + 1))
    barrier = pltpu.get_barrier_semaphore()
    pads = (pad_0, pad_1, pad_2)
    for pad in pads:
        fields = pad.shape[0]
        for x in (0, nx + 1):
            pad[:, x] = jnp.zeros((fields, ny, nz), jnp.float32)
    edge_in[...] = jnp.zeros(edge_in.shape, jnp.float32)
    for side in range(4):

        @pl.when(exists[side])
        def _(side=side):
            pl.semaphore_signal(barrier, inc=1, device_id=partner[side], device_id_type=MESH)

    pad_0[:, 1 : nx + 1] = state_ref[...]
    pl.semaphore_wait(barrier, sum(there.astype(jnp.int32) for there in exists))

    row = lax.broadcasted_iota(jnp.int32, (ny, nz), 0)
    column = lax.broadcasted_iota(jnp.int32, (ny, nz), 1)

    def copy_of(turn, side):
        pad = pads[turn]
        fields = pad.shape[0]
        if side == 0:
            source, target = pad.at[:, 1], pad.at[:, nx + 1]
        elif side == 1:
            source, target = pad.at[:, nx], pad.at[:, 0]
        else:
            source = edge_out.at[turn, side - 2, pl.ds(0, fields)]
            target = edge_in.at[turn, 3 - side, pl.ds(0, fields)]
        return pltpu.make_async_remote_copy(
            src_ref=source,
            dst_ref=target,
            send_sem=send_sems.at[turn, side],
            recv_sem=recv_sems.at[turn, side ^ 1],
            device_id=partner[side],
            device_id_type=MESH,
        )

    def arrival_of(turn, side):
        pad = pads[turn]
        fields = pad.shape[0]
        if side < 2:
            target = pad.at[:, 0 if side == 0 else nx + 1]
        else:
            target = edge_in.at[turn, side - 2, pl.ds(0, fields)]
        return pltpu.make_async_remote_copy(
            src_ref=target,
            dst_ref=target,
            send_sem=send_sems.at[turn, side],
            recv_sem=recv_sems.at[turn, side],
            device_id=partner[side],
            device_id_type=MESH,
        )

    for turn in range(SWEEPS):
        pad = pads[turn]
        for side in range(2):

            @pl.when(exists[side])
            def _(side=side):
                copy_of(turn, side).start()

        for field in range(pad.shape[0]):
            edge_out[turn, 0, field] = pad[field, 1 : nx + 1, 0, :]
            edge_out[turn, 1, field] = pad[field, 1 : nx + 1, ny - 1, :]
        for side in range(2, 4):

            @pl.when(exists[side])
            def _(side=side):
                copy_of(turn, side).start()

        for side in range(4):

            @pl.when(exists[side])
            def _(side=side):
                arrival_of(turn, side).wait_recv()

        def slab(x, carry, turn=turn, pad=pad):
            def around(ref, edges, field):
                centre = ref[field, x + 1]
                low = edges[0, field, pl.ds(x, 1), :]
                high = edges[1, field, pl.ds(x, 1), :]
                return (
                    centre,
                    ref[field, x + 2],
                    ref[field, x],
                    jnp.where(row == ny - 1, high, pltpu.roll(centre, ny - 1, 0)),
                    jnp.where(row == 0, low, pltpu.roll(centre, 1, 0)),
                    jnp.where(column == nz - 1, 0.0, pltpu.roll(centre, nz - 1, 1)),
                    jnp.where(column == 0, 0.0, pltpu.roll(centre, 1, 1)),
                )

            eta = around(pad_0, edge_in.at[0], 4)
            face = [0.5 * (eta[0] + eta[m]) for m in range(1, 7)]
            diagonal = face[0]
            for m in range(1, 6):
                diagonal = diagonal + face[m]
            scale = RELAX_WEIGHT / diagonal
            press = around(pad, edge_in.at[turn], 3)
            divergence = None
            for component in range(3):
                speed = around(pad, edge_in.at[turn], component)
                residual = face[0] * (speed[1] - speed[0])
                for m in range(1, 6):
                    residual = residual + face[m] * (speed[m + 1] - speed[0])
                up, down = 2 * component + 1, 2 * component + 2
                residual = residual - 0.5 * (press[up] - press[down])
                if component == 2:
                    residual = residual + DENSITY_FACTOR * heat_ref[x]
                moved = speed[0] + residual * scale
                if turn < SWEEPS - 1:
                    pads[turn + 1][component, x + 1] = moved
                else:
                    velocity_ref[component, x] = moved
                flux = 0.5 * (speed[up] - speed[down])
                divergence = flux if divergence is None else divergence + flux
            moved = press[0] - PRESSURE_WEIGHT * eta[0] * divergence
            if turn < SWEEPS - 1:
                pads[turn + 1][3, x + 1] = moved
            else:
                pressure_ref[x] = moved
            return carry

        lax.fori_loop(0, nx, slab, 0)

    for turn in range(SWEEPS):
        for side in range(4):

            @pl.when(exists[side])
            def _(turn=turn, side=side):
                copy_of(turn, side).wait_send()


def sweeps(state, heat):
    nx, ny, nz = heat.shape
    vmem = pl.BlockSpec(memory_space=pltpu.VMEM)
    return pl.pallas_call(
        functools.partial(
            sweep_kernel,
            wide_count=lax.axis_size("wide"),
            narrow_count=lax.axis_size("narrow"),
        ),
        out_shape=(
            jax.ShapeDtypeStruct((3, nx, ny, nz), jnp.float32),
            jax.ShapeDtypeStruct((nx, ny, nz), jnp.float32),
        ),
        in_specs=[vmem, vmem],
        out_specs=(vmem, vmem),
        scratch_shapes=[
            pltpu.VMEM((5, nx + 2, ny, nz), jnp.float32),
            pltpu.VMEM((4, nx + 2, ny, nz), jnp.float32),
            pltpu.VMEM((4, nx + 2, ny, nz), jnp.float32),
            pltpu.VMEM((SWEEPS, 2, 5, nx, nz), jnp.float32),
            pltpu.VMEM((SWEEPS, 2, 5, nx, nz), jnp.float32),
            pltpu.SemaphoreType.DMA((SWEEPS, 4)),
            pltpu.SemaphoreType.DMA((SWEEPS, 4)),
        ],
        compiler_params=pltpu.CompilerParams(
            collective_id=1, has_side_effects=True, vmem_limit_bytes=32 * 1024 * 1024
        ),
    )(state, heat)


def per_device(
    tile_flow_speed,
    tile_stress_mean,
    tile_heat_state,
    tile_drag_coefficient,
    marker_attributes,
    marker_holding_tile,
    marker_voxel_number,
    prior_slot_of_tile,
):
    wide_count = lax.axis_size("wide")
    narrow_count = lax.axis_size("narrow")
    device_count = wide_count * narrow_count
    my_index = lax.axis_index("wide") * narrow_count + lax.axis_index("narrow")
    blocks = prior_slot_of_tile.shape[0]
    props = marker_attributes.shape[0]
    everything = lax.all_gather(prior_slot_of_tile, ("wide", "narrow"), axis=0, tiled=True)
    local_old = everything.reshape(device_count, blocks) - my_index * blocks
    is_mine = (local_old >= 0) & (local_old < blocks)
    block_for = jnp.sum(jnp.where(is_mine, local_old, 0), axis=1)
    stacked = jnp.concatenate(
        [
            tile_flow_speed.reshape(blocks, 96, 128),
            tile_stress_mean.reshape(blocks, 32, 128),
            tile_heat_state.reshape(blocks, 32, 128),
            tile_drag_coefficient.reshape(blocks, 32, 128),
        ],
        axis=1,
    )
    received = lax.all_to_all(
        pick(block_for, stacked), ("wide", "narrow"), split_axis=0, concat_axis=0, tiled=True
    )
    means = bin_means(
        my_index * blocks, marker_holding_tile, marker_voxel_number, marker_attributes, blocks
    )
    by_block = means.reshape(props, blocks, BINS).transpose(1, 0, 2).reshape(blocks, 4, 128)
    received_means = lax.all_to_all(
        pick(block_for, by_block), ("wide", "narrow"), split_axis=0, concat_axis=0, tiled=True
    )
    source_dev = prior_slot_of_tile // blocks
    arrived = pick(source_dev, received_means).reshape(LX, LY, LZ, props, 4, 4, 4)
    bin_mean_attributes = arrived.transpose(3, 0, 4, 1, 5, 2, 6)
    bin_mean_attributes = bin_mean_attributes.reshape(props, LX * 4, LY * 4, LZ * 4)
    mixture = MIX_WEIGHTS[0] * bin_mean_attributes[0]
    for index_p in range(1, props):
        mixture = mixture + MIX_WEIGHTS[index_p] * bin_mean_attributes[index_p]
    state, heat = unpack(source_dev, received, mixture.reshape(LY * BS, LZ * 4))
    velocity, pressure = sweeps(state, heat)
    return (velocity, pressure, heat, bin_mean_attributes)


def solution(mesh):
    in_specs = (
        P(("wide", "narrow"), None, None),
        P(("wide", "narrow"), None),
        P(("wide", "narrow"), None),
        P(("wide", "narrow"), None),
        P(None, ("wide", "narrow")),
        P(("wide", "narrow")),
        P(("wide", "narrow")),
        P(("wide", "narrow")),
    )
    out_specs = (
        P(None, "wide", "narrow", None),
        P("wide", "narrow", None),
        P("wide", "narrow", None),
        P(None, "wide", "narrow", None),
    )
    return jax.shard_map(
        per_device, mesh=mesh, in_specs=in_specs, out_specs=out_specs, check_vma=False
    )
```

profile of v0, /device:TPU:3, one launch (start us, length us, event | category | flops | bytes accessed | tf_op | source)
XLA Modules:
  0.0 264.8 jit_solution(10855964300863814502)
XLA Ops:
  0.6 0.9 dynamic-update-slice
  1.5 39.6 %all-reduce = s32[512]{0:T(512)S(1)} all-reduce(s32[512]{0:T(512)S(1)} %dynamic-update-slice), channel_id=1, replica_groups=mesh['wide'=8,'narrow'=4] {'wide','narrow'}, use_global_device_ids=true, to_apply=%add | all-reduce | flops 512 | bytes 4096
  41.1 0.1 sub.16
  41.2 0.6 select_reduce_fusion.index_ref
  41.8 0.0 copy-start.2
  41.8 0.9 copy-done.2
  42.8 0.0 copy-start.3
  42.8 0.8 copy-done.3
  43.5 0.0 copy-start.4
  43.5 0.8 copy-done.4
  44.3 0.0 copy-start.6
  44.3 0.0 copy-start.7
  44.3 0.0 copy-start.8
  44.3 0.0 copy-start.5
  44.3 5.9 %shard_map.112 = f32[8,1024]{1,0:T(8,128)S(1)} custom-call(s32[1]{0:T(128)} %bitcast.base_ref, s32[1,8192]{1,0:T(1,128)S(1)} %bitcast.18, s32[1,8192]{1,0:T(1,128)S(1)} %bitcast.19, f32[8,8192]{1,0:T(8,128)S(1)} %copy-done.2), custom_call_target="tpu_custom_call" | custom-call | flops 536870912 | bytes 327680 | tf_op jit(solution)/shard_map/pallas_call | solution.py:63
  50.2 0.1 reshape.95
  50.3 0.7 reshape.96.from_ref
  51.0 4.0 %shard_map.113 = f32[32,4,128]{2,1,0:T(4,128)} custom-call(s32[32]{0:T(128)} %select_reduce_fusion.index_ref, f32[16,4,128]{2,1,0:T(4,128)} %reshape.96.from_ref), custom_call_target="tpu_custom_call" | custom-call | tf_op jit(solution)/shard_map/pallas_call | solution.py:102
  55.1 6.0 %all-to-all-start.1 = ((f32[32,4,128]{2,1,0:T(4,128)}), f32[32,4,128]{2,1,0:T(4,128)S(1)}, u32[]{:S(2)}, u32[]{:S(2)}) async-start(f32[32,4,128]{2,1,0:T(4,128)} %shard_map.113), calls=%async_computation.1 | async-start | bytes 131072 | tf_op jit(solution)/shard_map/all_to_all | solution.py:383
  61.1 0.0 copy-done.6
  61.1 0.1 copy.23
  61.1 0.0 copy-done.7
  61.2 0.1 copy.22
  61.2 0.0 copy-done.8
  61.2 0.1 copy.21
  61.3 0.0 copy-done.5
  61.3 0.5 copy.15
  61.8 0.6 reshape.88
  62.4 1.3 pad_maximum_fusion.from_ref
  63.7 97.3 %shard_map.111 = f32[32,192,128]{2,1,0:T(8,128)} custom-call(s32[32]{0:T(128)} %select_reduce_fusion.index_ref, f32[16,192,128]{2,1,0:T(8,128)} %pad_maximum_fusion.from_ref), custom_call_target="tpu_custom_call" | custom-call | tf_op jit(solution)/shard_map/pallas_call | solution.py:102
  161.0 0.0 copy-start.10
  161.1 0.0 all-to-all-done.1.from_ref
  161.1 0.0 copy-start.9
  161.1 0.6 copy-done.9
  161.7 5.8 %all-to-all-start = ((f32[32,192,128]{2,1,0:T(8,128)}), f32[32,192,128]{2,1,0:T(8,128)S(1)}, u32[]{:S(2)}, u32[]{:S(2)}) async-start(f32[32,192,128]{2,1,0:T(8,128)} %shard_map.111), calls=%async_computation | async-start | bytes 6291456 | tf_op jit(solution)/shard_map/all_to_all | solution.py:376
  167.5 0.0 copy-done.10
  167.6 0.5 and_select_fusion.index_ref.slot_ref
  168.1 2.9 %shard_map.114 = f32[16,4,128]{2,1,0:T(4,128)} custom-call(s32[16]{0:T(128)} %and_select_fusion.index_ref.slot_ref, f32[32,4,128]{2,1,0:T(4,128)} %copy-done.9), custom_call_target="tpu_custom_call" | custom-call | tf_op jit(solution)/shard_map/pallas_call | solution.py:102
  171.0 0.9 copy.17
  171.9 0.0 copy-start.1
  171.9 1.1 reshape.97
  173.0 2.1 copy.19
  175.1 1.3 fusion
  176.4 0.3 copy.18
  176.7 0.1 reshape.102.mix_ref
  176.8 1.9 copy.20
  178.7 60.3 %all-to-all-done.recv_ref = f32[32,192,128]{2,1,0:T(8,128)S(1)} async-done(((f32[32,192,128]{2,1,0:T(8,128)}), f32[32,192,128]{2,1,0:T(8,128)S(1)}, u32[]{:S(2)}, u32[]{:S(2)}) %all-to-all-start) | async-done | bytes 3145760 | tf_op jit(solution)/shard_map/all_to_all | solution.py:376
  238.9 0.0 copy-done.1
  238.9 5.4 %shard_map.115 = (f32[5,16,32,128]{3,2,1,0:T(8,128)S(1)}, f32[16,32,128]{2,1,0:T(8,128)}) custom-call(s32[16]{0:T(128)S(1)} %copy-done.1, f32[32,192,128]{2,1,0:T(8,128)S(1)} %all-to-all-done.recv_ref, f32[32,32]{1,0:T(8,128)S(1)} %reshape.102.mix_ref), custom_call_target="tpu_custom_call" | custom-call | tf_op jit(solution)/shard_map/pallas_call | solution.py:155
  244.3 0.0 copy-start
  244.4 0.9 copy-done
  245.3 17.9 %shard_map.116 = (f32[3,16,32,128]{3,2,1,0:T(8,128)S(1)}, f32[16,32,128]{2,1,0:T(8,128)S(1)}) custom-call(f32[5,16,32,128]{3,2,1,0:T(8,128)S(1)} %get-tuple-element.8.state_ref, f32[16,32,128]{2,1,0:T(8,128)S(1)} %copy-done), custom_call_target="tpu_custom_call" | custom-call | tf_op jit(solution)/shard_map/pallas_call | solution.py:320
  263.2 0.9 copy.29
  264.1 0.7 copy.30
  (3 shorter events, 0.0 us)
Async XLA Ops:
  41.8 0.9 copy-start.2
  42.8 0.8 copy-start.3
  43.5 0.8 copy-start.4
  44.3 16.8 %copy-start.6 = (f32[16,4096]{1,0:T(8,128)S(1)}, f32[16,4096]{1,0:T(8,128)}, u32[]{:S(2)}) copy-start(f32[16,4096]{1,0:T(8,128)} %param.11) | copy-start | bytes 786436
  44.3 16.9 %copy-start.7 = (f32[16,4096]{1,0:T(8,128)S(1)}, f32[16,4096]{1,0:T(8,128)}, u32[]{:S(2)}) copy-start(f32[16,4096]{1,0:T(8,128)} %param.10) | copy-start | bytes 786436
  44.3 16.9 %copy-start.8 = (f32[16,4096]{1,0:T(8,128)S(1)}, f32[16,4096]{1,0:T(8,128)}, u32[]{:S(2)}) copy-start(f32[16,4096]{1,0:T(8,128)} %param.9) | copy-start | bytes 786436
  44.3 17.0 %copy-start.5 = (f32[16,3,4096]{2,0,1:T(8,128)S(1)}, f32[16,3,4096]{2,0,1:T(8,128)}, u32[]{:S(2)}) copy-start(f32[16,3,4096]{2,0,1:T(8,128)} %param.8) | copy-start | bytes 2359300
  55.1 106.0 %all-to-all-start.1 = ((f32[32,4,128]{2,1,0:T(4,128)}), f32[32,4,128]{2,1,0:T(4,128)S(1)}, u32[]{:S(2)}, u32[]{:S(2)}) async-start(f32[32,4,128]{2,1,0:T(4,128)} %shard_map.113), calls=%async_computation.1 | async-start | bytes 131072 | tf_op jit(solution)/shard_map/all_to_all | solution.py:383
  161.0 6.5 %copy-start.10 = (s32[16]{0:T(128)S(1)}, s32[16]{0:T(128)}, u32[]{:S(2)}) copy-start(s32[16]{0:T(128)} %param.15) | copy-start | bytes 196
  161.1 0.6 copy-start.9
  161.7 77.2 %all-to-all-start = ((f32[32,192,128]{2,1,0:T(8,128)}), f32[32,192,128]{2,1,0:T(8,128)S(1)}, u32[]{:S(2)}, u32[]{:S(2)}) async-start(f32[32,192,128]{2,1,0:T(8,128)} %shard_map.111), calls=%async_computation | async-start | bytes 6291456 | tf_op jit(solution)/shard_map/all_to_all | solution.py:376
  171.9 67.1 %copy-start.1 = (s32[16]{0:T(128)S(1)}, s32[16]{0:T(128)}, u32[]{:S(2)}) copy-start(s32[16]{0:T(128)} %and_select_fusion.index_ref.slot_ref) | copy-start | bytes 196
  244.3 1.0 copy-start
where the time goes:
time: 265 us
  Pallas kernels  133 us (50%)
  waiting for transfers between devices  60.3 us (23%)
  blocking collectives  39.6 us (15%)
  local copies, waits for them, and re-layouts  15.1 us (6%)
  starting transfers between devices  11.8 us (4%)
  other arithmetic  3.67 us (1%)
    pallas_call x3, Pallas kernels, pick(): pl.pallas_call(pick_kernel, out_shape=jax.ShapeDtypeStruct(index.shape +...  104 us
    all_to_all x1, waiting for transfers between devices, per_device(): lax.all_to_all(pick(block_for, stacked), ('wide', 'narrow'), split_axis=0...  60.3 us
    unnamed x1, blocking collectives  39.6 us
    pallas_call x1, Pallas kernels, sweeps(): pl.pallas_call(functools.partial(sweep_kernel, wide_count=lax.axis_size('...  17.9 us
    unnamed x31, local copies, waits for them, and re-layouts  9.1 us
    all_to_all x1, starting transfers between devices, per_device(): lax.all_to_all(pick(block_for, by_block), ('wide', 'narrow'), split_axis=...  5.97 us
    pallas_call x1, Pallas kernels, bin_means(): pl.pallas_call(functools.partial(bin_kernel, blocks=blocks, chunk=chunk),...  5.94 us
    all_to_all x1, starting transfers between devices, per_device(): lax.all_to_all(pick(block_for, stacked), ('wide', 'narrow'), split_axis=0...  5.83 us
  transfers between devices with their start and end apart: 2, of which 1 were waited for; matrix products, arithmetic and copies ran while one was open for 4% of the time, Pallas kernels for 38%

commit v1 on v0

--- a/solution.py
+++ b/solution.py
@@ -20,6 +20,77 @@
 HEAT_FACTOR = 2.0
 DENSITY_FACTOR = 4.0
 MESH = pl.DeviceIdType.MESH
+
+
+def choose_kernel(
+    mine_ref, block_ref, table, send_sems, recv_sems, *, wide_count, narrow_count, blocks
+):
+    count = wide_count * narrow_count
+    me = lax.axis_index("wide") * narrow_count + lax.axis_index("narrow")
+
+    def place(step):
+        return lax.rem(me + step, count)
+
+    def coordinates(step):
+        other = place(step)
+        return (lax.div(other, narrow_count), lax.rem(other, narrow_count))
+
+    barrier = pltpu.get_barrier_semaphore()
+
+    def greet(step, carry):
+        pl.semaphore_signal(barrier, inc=1, device_id=coordinates(step), device_id_type=MESH)
+        return carry
+
+    lax.fori_loop(1, count, greet, 0)
+    pl.semaphore_wait(barrier, count - 1)
+
+    def copy_of(step, target):
+        return pltpu.make_async_remote_copy(
+            src_ref=mine_ref.at[0],
+            dst_ref=table.at[target],
+            send_sem=send_sems.at[step],
+            recv_sem=recv_sems.at[step],
+            device_id=coordinates(step),
+            device_id_type=MESH,
+        )
+
+    def send(step, carry):
+        copy_of(step, me).start()
+        return carry
+
+    lax.fori_loop(1, count, send, 0)
+    table[me] = mine_ref[0]
+
+    def finish(step, carry):
+        copy_of(step, place(count - step)).wait_recv()
+        copy_of(step, me).wait_send()
+        return carry
+
+    lax.fori_loop(1, count, finish, 0)
+    local_old = table[...] - me * blocks
+    is_mine = (local_old >= 0) & (local_old < blocks)
+    block_ref[...] = jnp.sum(jnp.where(is_mine, local_old, 0), axis=2)
+
+
+def choose_blocks(prior_slots):
+    wide_count, narrow_count = lax.axis_size("wide"), lax.axis_size("narrow")
+    count, blocks = wide_count * narrow_count, prior_slots.shape[0]
+    padded = jnp.pad(prior_slots, (0, 128 - blocks), constant_values=-1).reshape(1, 1, 128)
+    vmem = pl.BlockSpec(memory_space=pltpu.VMEM)
+    return pl.pallas_call(
+        functools.partial(
+            choose_kernel, wide_count=wide_count, narrow_count=narrow_count, blocks=blocks
+        ),
+        out_shape=jax.ShapeDtypeStruct((count, 1), jnp.int32),
+        in_specs=[vmem],
+        out_specs=vmem,
+        scratch_shapes=[
+            pltpu.VMEM((count, 1, 128), jnp.int32),
+            pltpu.SemaphoreType.DMA((count,)),
+            pltpu.SemaphoreType.DMA((count,)),
+        ],
+        compiler_params=pltpu.CompilerParams(collective_id=2, has_side_effects=True),
+    )(padded).reshape(count)
 
 
 def bin_kernel(base_ref, holder_ref, voxel_ref, attr_ref, mean_ref, *, blocks, chunk):
@@ -104,10 +175,11 @@
         out_shape=jax.ShapeDtypeStruct(index.shape + array.shape[1:], array.dtype),
         in_specs=[
             pl.BlockSpec(memory_space=pltpu.SMEM),
-            pl.BlockSpec(memory_space=pl.ANY),
+            pl.BlockSpec(memory_space=pltpu.VMEM),
         ],
         out_specs=pl.BlockSpec(memory_space=pl.ANY),
         scratch_shapes=[pltpu.SemaphoreType.DMA(index.shape)],
+        compiler_params=pltpu.CompilerParams(vmem_limit_bytes=32 * 1024 * 1024),
     )(index, array)
 
 
@@ -356,14 +428,10 @@
 ):
     wide_count = lax.axis_size("wide")
     narrow_count = lax.axis_size("narrow")
-    device_count = wide_count * narrow_count
     my_index = lax.axis_index("wide") * narrow_count + lax.axis_index("narrow")
     blocks = prior_slot_of_tile.shape[0]
     props = marker_attributes.shape[0]
-    everything = lax.all_gather(prior_slot_of_tile, ("wide", "narrow"), axis=0, tiled=True)
-    local_old = everything.reshape(device_count, blocks) - my_index * blocks
-    is_mine = (local_old >= 0) & (local_old < blocks)
-    block_for = jnp.sum(jnp.where(is_mine, local_old, 0), axis=1)
+    block_for = choose_blocks(prior_slot_of_tile)
     stacked = jnp.concatenate(
         [
             tile_flow_speed.reshape(blocks, 96, 128),
@@ -373,8 +441,10 @@
         ],
         axis=1,
     )
+    outgoing = pick(block_for, stacked)
+    outgoing, marker_attributes = lax.optimization_barrier((outgoing, marker_attributes))
     received = lax.all_to_all(
-        pick(block_for, stacked), ("wide", "narrow"), split_axis=0, concat_axis=0, tiled=True
+        outgoing, ("wide", "narrow"), split_axis=0, concat_axis=0, tiled=True
     )
     means = bin_means(
         my_index * blocks, marker_holding_tile, marker_voxel_number, marker_attributes, blocks

time: 265 us -> 140 us (0.53)
  Pallas kernels: 133 us -> 43.2 us
  blocking collectives: 39.6 us -> 11.8 us
  starting transfers between devices: 11.8 us -> 4.19 us
  waiting for transfers between devices: 60.3 us -> 63.8 us
    pallas_call x3, Pallas kernels: 104 us -> 4.31 us  [pick(): pl.pallas_call(pick_kernel, out_shape=jax.ShapeDtypeStruct(index.shape +...]
    unnamed x1 -> x0, blocking collectives: 39.6 us -> none
    all_to_all x0 -> x1, blocking collectives: none -> 11.8 us  [per_device(): lax.all_to_all(pick(block_for, by_block), ('wide', 'narrow'), split_axis=...]
    pallas_call x0 -> x1, Pallas kernels: none -> 9.73 us  [choose_blocks(): pl.pallas_call(functools.partial(choose_kernel, wide_count=wide_count, na...]
    all_to_all x2 -> x1, starting transfers between devices: 11.8 us -> 4.19 us  [per_device(): lax.all_to_all(outgoing, ('wide', 'narrow'), split_axis=0, concat_axis=0,...]
    all_to_all x2 -> x1, waiting for transfers between devices: 60.3 us -> 63.8 us  [per_device(): lax.all_to_all(outgoing, ('wide', 'narrow'), split_axis=0, concat_axis=0,...]
    unnamed x31 -> x21, local copies, waits for them, and re-layouts: 9.1 us -> 8.01 us
  transfers between devices with their start and end apart: 2 -> 1, of which waited for: 1 -> 1; matrix products, arithmetic and copies ran while one was open for 4% -> 5% of each run, Pallas kernels for 38% -> 1%
where the time goes in v1:
time: 140 us; the launch traced here: 139 us
  waiting for transfers between devices  63.8 us (46%)
  Pallas kernels  43.2 us (31%)
  local copies, waits for them, and re-layouts  13.8 us (10%)
  blocking collectives  11.8 us (8%)
  starting transfers between devices  4.19 us (3%)
  other arithmetic  1.49 us (1%)
    all_to_all x1, waiting for transfers between devices, per_device(): lax.all_to_all(outgoing, ('wide', 'narrow'), split_axis=0, concat_axis=0,...  63.8 us
    pallas_call x1, Pallas kernels, sweeps(): pl.pallas_call(functools.partial(sweep_kernel, wide_count=lax.axis_size('...  17.8 us
    all_to_all x1, blocking collectives, per_device(): lax.all_to_all(pick(block_for, by_block), ('wide', 'narrow'), split_axis=...  11.8 us
    pallas_call x1, Pallas kernels, choose_blocks(): pl.pallas_call(functools.partial(choose_kernel, wide_count=wide_count, na...  9.73 us
    unnamed x21, local copies, waits for them, and re-layouts  8.01 us
    pallas_call x1, Pallas kernels, bin_means(): pl.pallas_call(functools.partial(bin_kernel, blocks=blocks, chunk=chunk),...  5.93 us
    pallas_call x1, Pallas kernels, unpack(): pl.pallas_call(unpack_kernel, out_shape=(jax.ShapeDtypeStruct((5,) + grid...  5.39 us
    pallas_call x3, Pallas kernels, pick(): pl.pallas_call(pick_kernel, out_shape=jax.ShapeDtypeStruct(index.shape +...  4.31 us
  transfers between devices with their start and end apart: 1, of which 1 were waited for; matrix products, arithmetic and copies ran while one was open for 5% of the time, Pallas kernels for 1%

profile of v1, /device:TPU:3, one launch (start us, length us, event | category | flops | bytes accessed | tf_op | source)
XLA Modules:
  0.0 139.2 jit_solution(16915192457340911944)
XLA Ops:
  0.6 0.0 copy-start.4
  0.6 1.2 pad_bitcast_fusion.mine_ref
  1.9 9.7 %shard_map.111 = s32[32,1]{1,0:T(8,128)} custom-call(s32[1,1,128]{2,1,0:T(1,128)} %pad_bitcast_fusion.mine_ref), custom_call_target="tpu_custom_call" | custom-call | tf_op jit(solution)/shard_map/pallas_call | solution.py:80
  11.6 1.0 copy.23
  12.6 1.0 copy.22
  13.6 1.0 copy.21
  14.6 0.0 copy-done.4
  14.7 0.0 copy-start.5
  14.7 0.5 copy.15
  15.2 0.6 reshape.93
  15.8 0.0 copy-done.5
  15.8 0.1 reduce.index_ref
  15.9 0.1 pad_maximum_fusion.from_ref
  16.1 0.0 copy-start.1
  16.1 0.0 copy-start.2
  16.1 0.0 copy-start.3
  16.1 2.5 %shard_map.112 = f32[32,192,128]{2,1,0:T(8,128)} custom-call(s32[32]{0:T(128)S(1)} %reduce.index_ref, f32[16,192,128]{2,1,0:T(8,128)S(1)} %pad_maximum_fusion.from_ref), custom_call_target="tpu_custom_call" | custom-call | tf_op jit(solution)/shard_map/pallas_call | solution.py:173
  18.6 0.0 copy-done.1
  18.6 0.0 copy-done.2
  18.6 0.0 copy-done.3
  18.6 5.9 %shard_map.113 = f32[8,1024]{1,0:T(8,128)S(1)} custom-call(s32[1]{0:T(128)} %bitcast.1.base_ref, s32[1,8192]{1,0:T(1,128)S(1)} %bitcast.20, s32[1,8192]{1,0:T(1,128)S(1)} %bitcast.21, f32[8,8192]{1,0:T(8,128)S(1)} %copy-done.1), custom_call_target="tpu_custom_call" | custom-call | flops 536870912 | bytes 327680 | tf_op jit(solution)/shard_map/pallas_call | solution.py:134
  24.5 0.1 reshape.100
  24.7 0.1 reshape.101.from_ref
  24.7 1.0 shard_map.114
  25.8 11.8 %all_to_all.10.from_ref = f32[32,4,128]{2,1,0:T(4,128)S(1)} all-to-all(f32[32,4,128]{2,1,0:T(4,128)S(1)} %shard_map.114), channel_id=1, replica_groups=mesh['wide'=8,'narrow'=4] {'wide','narrow'}, dimensions={0} | all-to-all | bytes 131072 | tf_op jit(solution)/shard_map/all_to_all | solution.py:453
  37.6 0.0 copy-start.6
  37.6 4.2 %all-to-all-start = ((f32[32,192,128]{2,1,0:T(8,128)}), f32[32,192,128]{2,1,0:T(8,128)S(1)}, u32[]{:S(2)}, u32[]{:S(2)}) async-start(f32[32,192,128]{2,1,0:T(8,128)} %shard_map.112), calls=%async_computation | async-start | bytes 6291456 | tf_op jit(solution)/shard_map/all_to_all | solution.py:446
  41.8 0.0 copy-done.6
  41.9 0.8 shard_map.115
  42.7 0.1 copy.17
  42.8 1.1 reshape.102
  43.9 2.1 %copy.19 = f32[8,1,4,2,4,8,4]{0,6,5,4,3,2,1:T(4,128)} copy(f32[8,1,4,2,4,8,4]{5,3,6,4,2,0,1:T(2,128)} %bitcast.22) | data formatting | bytes 65536 | tf_op jit(solution)/shard_map/transpose | solution.py:458
  46.0 1.3 fusion
  47.3 0.3 copy.18
  47.6 0.1 reshape.107.mix_ref
  47.7 1.9 %copy.20 = f32[8,4,8,32]{3,2,1,0:T(8,128)} copy(f32[8,4,8,32]{0,3,2,1:T(8,128)} %bitcast.24) | data formatting | bytes 65536
  49.6 63.8 %all-to-all-done.recv_ref = f32[32,192,128]{2,1,0:T(8,128)S(1)} async-done(((f32[32,192,128]{2,1,0:T(8,128)}), f32[32,192,128]{2,1,0:T(8,128)S(1)}, u32[]{:S(2)}, u32[]{:S(2)}) %all-to-all-start) | async-done | bytes 3145760 | tf_op jit(solution)/shard_map/all_to_all | solution.py:446
  113.4 5.4 %shard_map.116 = (f32[5,16,32,128]{3,2,1,0:T(8,128)S(1)}, f32[16,32,128]{2,1,0:T(8,128)}) custom-call(s32[16]{0:T(128)S(1)} %and_select_fusion.index_ref.slot_ref, f32[32,192,128]{2,1,0:T(8,128)S(1)} %all-to-all-done.recv_ref, f32[32,32]{1,0:T(8,128)S(1)} %reshape.107.mix_ref), custom_call_target="tpu_custom_call" | custom-call | tf_op jit(solution)/shard_map/pallas_call | solution.py:227
  118.8 0.0 copy-start
  118.8 0.9 copy-done
  119.7 17.8 %shard_map.117 = (f32[3,16,32,128]{3,2,1,0:T(8,128)S(1)}, f32[16,32,128]{2,1,0:T(8,128)S(1)}) custom-call(f32[5,16,32,128]{3,2,1,0:T(8,128)S(1)} %get-tuple-element.12.state_ref, f32[16,32,128]{2,1,0:T(8,128)S(1)} %copy-done), custom_call_target="tpu_custom_call" | custom-call | tf_op jit(solution)/shard_map/pallas_call | solution.py:392
  137.6 0.9 copy.28
  138.5 0.7 copy.29
  (2 shorter events, 0.0 us)
Async XLA Ops:
  0.6 14.0 %copy-start.4 = (f32[16,3,4096]{2,0,1:T(8,128)S(1)}, f32[16,3,4096]{2,0,1:T(8,128)}, u32[]{:S(2)}) copy-start(f32[16,3,4096]{2,0,1:T(8,128)} %param.8) | copy-start | bytes 2359300
  14.7 1.2 copy-start.5
  16.1 2.5 %copy-start.1 = (f32[8,8192]{1,0:T(8,128)S(1)}, f32[8,8192]{1,0:T(8,128)}, u32[]{:S(2)}) copy-start(f32[8,8192]{1,0:T(8,128)} %attr_ref) | copy-start | bytes 786436
  16.1 2.5 %copy-start.2 = (s32[8192]{0:T(1024)S(1)}, s32[8192]{0:T(1024)}, u32[]{:S(2)}) copy-start(s32[8192]{0:T(1024)} %param.13) | copy-start | bytes 98308
  16.1 2.5 %copy-start.3 = (s32[8192]{0:T(1024)S(1)}, s32[8192]{0:T(1024)}, u32[]{:S(2)}) copy-start(s32[8192]{0:T(1024)} %param.14) | copy-start | bytes 98308
  37.6 4.2 %copy-start.6 = (s32[16]{0:T(128)S(1)}, s32[16]{0:T(128)}, u32[]{:S(2)}) copy-start(s32[16]{0:T(128)} %param.15) | copy-start | bytes 196
  37.6 75.8 %all-to-all-start = ((f32[32,192,128]{2,1,0:T(8,128)}), f32[32,192,128]{2,1,0:T(8,128)S(1)}, u32[]{:S(2)}, u32[]{:S(2)}) async-start(f32[32,192,128]{2,1,0:T(8,128)} %shard_map.112), calls=%async_computation | async-start | bytes 6291456 | tf_op jit(solution)/shard_map/all_to_all | solution.py:446
  118.8 1.0 copy-start

commit v2 on v1

--- a/solution.py
+++ b/solution.py
@@ -91,6 +91,74 @@
         ],
         compiler_params=pltpu.CompilerParams(collective_id=2, has_side_effects=True),
     )(padded).reshape(count)
+
+
+def exchange_kernel(
+    send_ref, out_ref, landed, send_sems, recv_sems, *, wide_count, narrow_count
+):
+    count = wide_count * narrow_count
+    me = lax.axis_index("wide") * narrow_count + lax.axis_index("narrow")
+
+    def place(step):
+        return lax.rem(me + step, count)
+
+    def coordinates(step):
+        other = place(step)
+        return (lax.div(other, narrow_count), lax.rem(other, narrow_count))
+
+    barrier = pltpu.get_barrier_semaphore()
+
+    def greet(step, carry):
+        pl.semaphore_signal(barrier, inc=1, device_id=coordinates(step), device_id_type=MESH)
+        return carry
+
+    lax.fori_loop(1, count, greet, 0)
+    pl.semaphore_wait(barrier, count - 1)
+
+    def copy_of(step, target):
+        return pltpu.make_async_remote_copy(
+            src_ref=send_ref.at[place(step)],
+            dst_ref=landed.at[target],
+            send_sem=send_sems.at[step],
+            recv_sem=recv_sems.at[step],
+            device_id=coordinates(step),
+            device_id_type=MESH,
+        )
+
+    def send(step, carry):
+        copy_of(step, me).start()
+        return carry
+
+    lax.fori_loop(1, count, send, 0)
+    landed[me] = send_ref[me]
+
+    def finish(step, carry):
+        copy_of(step, place(count - step)).wait_recv()
+        copy_of(step, me).wait_send()
+        return carry
+
+    lax.fori_loop(1, count, finish, 0)
+    out_ref[...] = landed[...]
+
+
+def exchange(entries):
+    wide_count, narrow_count = lax.axis_size("wide"), lax.axis_size("narrow")
+    count = wide_count * narrow_count
+    vmem = pl.BlockSpec(memory_space=pltpu.VMEM)
+    return pl.pallas_call(
+        functools.partial(exchange_kernel, wide_count=wide_count, narrow_count=narrow_count),
+        out_shape=jax.ShapeDtypeStruct(entries.shape, entries.dtype),
+        in_specs=[vmem],
+        out_specs=vmem,
+        scratch_shapes=[
+            pltpu.VMEM(entries.shape, entries.dtype),
+            pltpu.SemaphoreType.DMA((count,)),
+            pltpu.SemaphoreType.DMA((count,)),
+        ],
+        compiler_params=pltpu.CompilerParams(
+            collective_id=3, has_side_effects=True, vmem_limit_bytes=32 * 1024 * 1024
+        ),
+    )(entries)
 
 
 def bin_kernel(base_ref, holder_ref, voxel_ref, attr_ref, mean_ref, *, blocks, chunk):
@@ -450,9 +518,7 @@
         my_index * blocks, marker_holding_tile, marker_voxel_number, marker_attributes, blocks
     )
     by_block = means.reshape(props, blocks, BINS).transpose(1, 0, 2).reshape(blocks, 4, 128)
-    received_means = lax.all_to_all(
-        pick(block_for, by_block), ("wide", "narrow"), split_axis=0, concat_axis=0, tiled=True
-    )
+    received_means = exchange(pick(block_for, by_block))
     source_dev = prior_slot_of_tile // blocks
     arrived = pick(source_dev, received_means).reshape(LX, LY, LZ, props, 4, 4, 4)
     bin_mean_attributes = arrived.transpose(3, 0, 4, 1, 5, 2, 6)

time: 140 us -> 138 us (0.986)
  Pallas kernels: 43.2 us -> 114 us
  waiting for transfers between devices: 63.8 us -> 0.01 us
  blocking collectives: 11.8 us -> 0 us
  starting transfers between devices: 4.19 us -> 5.94 us
  local copies, waits for them, and re-layouts: 13.8 us -> 15.4 us
    pallas_call x0 -> x1, Pallas kernels: none -> 68 us  [exchange(): pl.pallas_call(functools.partial(exchange_kernel, wide_count=wide_count,...]
    all_to_all x1, waiting for transfers between devices: 63.8 us -> 0.01 us  [per_device(): lax.all_to_all(outgoing, ('wide', 'narrow'), split_axis=0, concat_axis=0,...]
    all_to_all x1 -> x0, blocking collectives: 11.8 us -> none  [per_device(): lax.all_to_all(pick(block_for, by_block), ('wide', 'narrow'), split_axis=...]
    pallas_call x3, Pallas kernels: 4.31 us -> 6.9 us  [pick(): pl.pallas_call(pick_kernel, out_shape=jax.ShapeDtypeStruct(index.shape +...]
    all_to_all x1, starting transfers between devices: 4.19 us -> 5.94 us  [per_device(): lax.all_to_all(outgoing, ('wide', 'narrow'), split_axis=0, concat_axis=0,...]
    unnamed x21 -> x23, local copies, waits for them, and re-layouts: 8.01 us -> 9.63 us
  transfers between devices with their start and end apart: 1 -> 1, of which waited for: 1 -> 0; matrix products, arithmetic and copies ran while one was open for 5% -> 5% of each run, Pallas kernels for 1% -> 55%
where the time goes in v2:
time: 138 us
  Pallas kernels  114 us (83%)
  local copies, waits for them, and re-layouts  15.4 us (11%)
  starting transfers between devices  5.94 us (4%)
  other arithmetic  1.49 us (1%)
    pallas_call x1, Pallas kernels, exchange(): pl.pallas_call(functools.partial(exchange_kernel, wide_count=wide_count,...  68 us
    pallas_call x1, Pallas kernels, sweeps(): pl.pallas_call(functools.partial(sweep_kernel, wide_count=lax.axis_size('...  18.1 us
    pallas_call x1, Pallas kernels, choose_blocks(): pl.pallas_call(functools.partial(choose_kernel, wide_count=wide_count, na...  9.74 us
    unnamed x23, local copies, waits for them, and re-layouts  9.63 us
    pallas_call x3, Pallas kernels, pick(): pl.pallas_call(pick_kernel, out_shape=jax.ShapeDtypeStruct(index.shape +...  6.9 us
    all_to_all x1, starting transfers between devices, per_device(): lax.all_to_all(outgoing, ('wide', 'narrow'), split_axis=0, concat_axis=0,...  5.94 us
    pallas_call x1, Pallas kernels, bin_means(): pl.pallas_call(functools.partial(bin_kernel, blocks=blocks, chunk=chunk),...  5.93 us
    pallas_call x1, Pallas kernels, unpack(): pl.pallas_call(unpack_kernel, out_shape=(jax.ShapeDtypeStruct((5,) + grid...  5.39 us
  transfers between devices with their start and end apart: 1, of which 0 were waited for; matrix products, arithmetic and copies ran while one was open for 5% of the time, Pallas kernels for 55%

profile of v2, /device:TPU:3, one launch (start us, length us, event | category | flops | bytes accessed | tf_op | source)
XLA Modules:
  0.0 137.7 jit_solution(13364740277805493286)
XLA Ops:
  0.6 0.0 copy-start.5
  0.6 1.2 pad_bitcast_fusion.mine_ref
  1.9 9.7 %shard_map.111 = s32[32,1]{1,0:T(8,128)} custom-call(s32[1,1,128]{2,1,0:T(1,128)} %pad_bitcast_fusion.mine_ref), custom_call_target="tpu_custom_call" | custom-call | tf_op jit(solution)/shard_map/pallas_call | solution.py:80
  11.6 1.0 copy.23
  12.6 1.0 copy.22
  13.6 1.0 copy.21
  14.6 0.0 copy-done.5
  14.7 0.0 copy-start.6
  14.7 0.5 copy.15
  15.2 0.6 reshape.93
  15.8 0.0 copy-done.6
  15.8 0.1 reduce.index_ref
  15.9 0.1 pad_maximum_fusion.from_ref
  16.1 5.1 %shard_map.112 = f32[32,192,128]{2,1,0:T(8,128)S(1)} custom-call(s32[32]{0:T(128)S(1)} %reduce.index_ref, f32[16,192,128]{2,1,0:T(8,128)S(1)} %pad_maximum_fusion.from_ref), custom_call_target="tpu_custom_call" | custom-call | tf_op jit(solution)/shard_map/pallas_call | solution.py:241
  21.1 0.0 copy-start
  21.1 1.6 %copy-done = f32[32,192,128]{2,1,0:T(8,128)} copy-done((f32[32,192,128]{2,1,0:T(8,128)}, f32[32,192,128]{2,1,0:T(8,128)S(1)}, u32[]{:S(2)}) %copy-start) | copy-done | bytes 3145752
  22.8 0.0 copy-start.2
  22.8 0.0 copy-start.3
  22.8 0.0 copy-start.4
  22.8 5.9 %all-to-all-start = ((f32[32,192,128]{2,1,0:T(8,128)}), f32[32,192,128]{2,1,0:T(8,128)S(1)}, u32[]{:S(2)}, u32[]{:S(2)}) async-start(f32[32,192,128]{2,1,0:T(8,128)} %copy-done), calls=%async_computation | async-start | bytes 6291456 | tf_op jit(solution)/shard_map/all_to_all | solution.py:514
  28.7 0.0 copy-start.7
  28.7 0.0 copy-done.2
  28.7 0.0 copy-done.3
  28.7 0.0 copy-done.4
  28.8 5.9 %shard_map.113 = f32[8,1024]{1,0:T(8,128)S(1)} custom-call(s32[1]{0:T(128)} %bitcast.1.base_ref, s32[1,8192]{1,0:T(1,128)S(1)} %bitcast.20, s32[1,8192]{1,0:T(1,128)S(1)} %bitcast.21, f32[8,8192]{1,0:T(8,128)S(1)} %copy-done.2), custom_call_target="tpu_custom_call" | custom-call | flops 536870912 | bytes 327680 | tf_op jit(solution)/shard_map/pallas_call | solution.py:202
  34.7 0.1 reshape.100
  34.8 0.1 reshape.101.from_ref
  34.9 1.0 shard_map.114.send_ref
  35.9 68.0 %shard_map.115.from_ref = f32[32,4,128]{2,1,0:T(4,128)S(1)} custom-call(f32[32,4,128]{2,1,0:T(4,128)S(1)} %shard_map.114.send_ref), custom_call_target="tpu_custom_call" | custom-call | tf_op jit(solution)/shard_map/pallas_call | solution.py:148
  103.9 0.0 copy-done.7
  104.0 0.8 shard_map.116
  104.8 0.1 copy.17
  104.9 1.1 reshape.102
  106.0 2.1 %copy.19 = f32[8,1,4,2,4,8,4]{0,6,5,4,3,2,1:T(4,128)} copy(f32[8,1,4,2,4,8,4]{5,3,6,4,2,0,1:T(2,128)} %bitcast.22) | data formatting | bytes 65536 | tf_op jit(solution)/shard_map/transpose | solution.py:524
  108.1 1.3 fusion
  109.4 0.3 copy.18
  109.7 0.1 reshape.107.mix_ref
  109.8 1.9 %copy.20 = f32[8,4,8,32]{3,2,1,0:T(8,128)} copy(f32[8,4,8,32]{0,3,2,1:T(8,128)} %bitcast.24) | data formatting | bytes 65536
  111.7 0.0 all-to-all-done.recv_ref
  111.7 5.4 %shard_map.117 = (f32[5,16,32,128]{3,2,1,0:T(8,128)S(1)}, f32[16,32,128]{2,1,0:T(8,128)}) custom-call(s32[16]{0:T(128)S(1)} %and_select_fusion.index_ref.slot_ref, f32[32,192,128]{2,1,0:T(8,128)S(1)} %all-to-all-done.recv_ref, f32[32,32]{1,0:T(8,128)S(1)} %reshape.107.mix_ref), custom_call_target="tpu_custom_call" | custom-call | tf_op jit(solution)/shard_map/pallas_call | solution.py:295
  117.1 0.0 copy-start.1
  117.1 0.9 copy-done.1
  118.0 18.1 %shard_map.118 = (f32[3,16,32,128]{3,2,1,0:T(8,128)S(1)}, f32[16,32,128]{2,1,0:T(8,128)S(1)}) custom-call(f32[5,16,32,128]{3,2,1,0:T(8,128)S(1)} %get-tuple-element.12.state_ref, f32[16,32,128]{2,1,0:T(8,128)S(1)} %copy-done.1), custom_call_target="tpu_custom_call" | custom-call | tf_op jit(solution)/shard_map/pallas_call | solution.py:460
  136.1 0.9 copy.28
  137.0 0.7 copy.29
  (2 shorter events, 0.0 us)
Async XLA Ops:
  0.6 14.0 %copy-start.5 = (f32[16,3,4096]{2,0,1:T(8,128)S(1)}, f32[16,3,4096]{2,0,1:T(8,128)}, u32[]{:S(2)}) copy-start(f32[16,3,4096]{2,0,1:T(8,128)} %param.8) | copy-start | bytes 2359300
  14.7 1.2 copy-start.6
  21.1 1.6 %copy-start = (f32[32,192,128]{2,1,0:T(8,128)}, f32[32,192,128]{2,1,0:T(8,128)S(1)}, u32[]{:S(2)}) copy-start(f32[32,192,128]{2,1,0:T(8,128)S(1)} %shard_map.112) | copy-start | bytes 9437188
  22.8 6.0 %copy-start.2 = (f32[8,8192]{1,0:T(8,128)S(1)}, f32[8,8192]{1,0:T(8,128)}, u32[]{:S(2)}) copy-start(f32[8,8192]{1,0:T(8,128)} %attr_ref) | copy-start | bytes 786436
  22.8 6.0 %copy-start.3 = (s32[8192]{0:T(1024)S(1)}, s32[8192]{0:T(1024)}, u32[]{:S(2)}) copy-start(s32[8192]{0:T(1024)} %param.13) | copy-start | bytes 98308
  22.8 6.0 %copy-start.4 = (s32[8192]{0:T(1024)S(1)}, s32[8192]{0:T(1024)}, u32[]{:S(2)}) copy-start(s32[8192]{0:T(1024)} %param.14) | copy-start | bytes 98308
  22.8 88.9 %all-to-all-start = ((f32[32,192,128]{2,1,0:T(8,128)}), f32[32,192,128]{2,1,0:T(8,128)S(1)}, u32[]{:S(2)}, u32[]{:S(2)}) async-start(f32[32,192,128]{2,1,0:T(8,128)} %copy-done), calls=%async_computation | async-start | bytes 6291456 | tf_op jit(solution)/shard_map/all_to_all | solution.py:514
  28.7 75.2 %copy-start.7 = (s32[16]{0:T(128)S(1)}, s32[16]{0:T(128)}, u32[]{:S(2)}) copy-start(s32[16]{0:T(128)} %param.15) | copy-start | bytes 196
  117.1 1.0 copy-start.1

commit v3 on v2

--- a/solution.py
+++ b/solution.py
@@ -444,7 +444,7 @@
                 pressure_ref[x] = moved
             return carry
 
-        lax.fori_loop(0, nx, slab, 0)
+        lax.fori_loop(0, nx, slab, 0, unroll=2)
 
     for turn in range(SWEEPS):
         for side in range(4):
@@ -510,15 +510,15 @@
         axis=1,
     )
     outgoing = pick(block_for, stacked)
-    outgoing, marker_attributes = lax.optimization_barrier((outgoing, marker_attributes))
+    means = bin_means(
+        my_index * blocks, marker_holding_tile, marker_voxel_number, marker_attributes, blocks
+    )
+    by_block = means.reshape(props, blocks, BINS).transpose(1, 0, 2).reshape(blocks, 4, 128)
+    received_means = exchange(pick(block_for, by_block))
+    outgoing, received_means = lax.optimization_barrier((outgoing, received_means))
     received = lax.all_to_all(
         outgoing, ("wide", "narrow"), split_axis=0, concat_axis=0, tiled=True
     )
-    means = bin_means(
-        my_index * blocks, marker_holding_tile, marker_voxel_number, marker_attributes, blocks
-    )
-    by_block = means.reshape(props, blocks, BINS).transpose(1, 0, 2).reshape(blocks, 4, 128)
-    received_means = exchange(pick(block_for, by_block))
     source_dev = prior_slot_of_tile // blocks
     arrived = pick(source_dev, received_means).reshape(LX, LY, LZ, props, 4, 4, 4)
     bin_mean_attributes = arrived.transpose(3, 0, 4, 1, 5, 2, 6)

time: 138 us -> 140 us (1.014)
  waiting for transfers between devices: 0.01 us -> 63.7 us
  Pallas kernels: 114 us -> 53.4 us
    all_to_all x1, waiting for transfers between devices: 0.01 us -> 63.7 us  [per_device(): lax.all_to_all(outgoing, ('wide', 'narrow'), split_axis=0, concat_axis=0,...]
    pallas_call x1, Pallas kernels: 68 us -> 9.07 us  [exchange(): pl.pallas_call(functools.partial(exchange_kernel, wide_count=wide_count,...]
    pallas_call x1, Pallas kernels: 18.1 us -> 16.4 us  [sweeps(): pl.pallas_call(functools.partial(sweep_kernel, wide_count=lax.axis_size('...]
    unnamed x23 -> x29, local copies, waits for them, and re-layouts: 9.63 us -> 9.23 us
  transfers between devices with their start and end apart: 1 -> 1, of which waited for: 0 -> 1; matrix products, arithmetic and copies ran while one was open for 5% -> 5% of each run, Pallas kernels for 55% -> 1%
where the time goes in v3:
time: 140 us
  waiting for transfers between devices  63.7 us (46%)
  Pallas kernels  53.4 us (38%)
  local copies, waits for them, and re-layouts  14.9 us (11%)
  starting transfers between devices  5.19 us (4%)
  other arithmetic  1.48 us (1%)
    all_to_all x1, waiting for transfers between devices, per_device(): lax.all_to_all(outgoing, ('wide', 'narrow'), split_axis=0, concat_axis=0,...  63.7 us
    pallas_call x1, Pallas kernels, sweeps(): pl.pallas_call(functools.partial(sweep_kernel, wide_count=lax.axis_size('...  16.4 us
    pallas_call x1, Pallas kernels, choose_blocks(): pl.pallas_call(functools.partial(choose_kernel, wide_count=wide_count, na...  9.73 us
    unnamed x29, local copies, waits for them, and re-layouts  9.23 us
    pallas_call x1, Pallas kernels, exchange(): pl.pallas_call(functools.partial(exchange_kernel, wide_count=wide_count,...  9.07 us
    pallas_call x3, Pallas kernels, pick(): pl.pallas_call(pick_kernel, out_shape=jax.ShapeDtypeStruct(index.shape +...  6.9 us
    pallas_call x1, Pallas kernels, bin_means(): pl.pallas_call(functools.partial(bin_kernel, blocks=blocks, chunk=chunk),...  5.94 us
    pallas_call x1, Pallas kernels, unpack(): pl.pallas_call(unpack_kernel, out_shape=(jax.ShapeDtypeStruct((5,) + grid...  5.39 us
  transfers between devices with their start and end apart: 1, of which 1 were waited for; matrix products, arithmetic and copies ran while one was open for 5% of the time, Pallas kernels for 1%

profile of v3, /device:TPU:3, one launch (start us, length us, event | category | flops | bytes accessed | tf_op | source)
XLA Modules:
  0.0 139.5 jit_solution(1747850030994104046)
XLA Ops:
  0.6 1.2 pad_bitcast_fusion.mine_ref
  1.8 9.7 %shard_map.111 = s32[32,1]{1,0:T(8,128)} custom-call(s32[1,1,128]{2,1,0:T(1,128)} %pad_bitcast_fusion.mine_ref), custom_call_target="tpu_custom_call" | custom-call | tf_op jit(solution)/shard_map/pallas_call | solution.py:80
  11.6 0.0 copy-start.2
  11.6 0.9 copy-done.2
  12.5 0.0 copy-start.3
  12.5 0.8 copy-done.3
  13.3 0.0 copy-start.4
  13.3 0.8 copy-done.4
  14.0 0.0 copy-start.9
  14.0 0.0 copy-start.6
  14.0 0.0 copy-start.7
  14.0 0.0 copy-start.8
  14.0 5.9 %shard_map.113 = f32[8,1024]{1,0:T(8,128)S(1)} custom-call(s32[1]{0:T(128)} %bitcast.1.base_ref, s32[1,8192]{1,0:T(1,128)S(1)} %bitcast.20, s32[1,8192]{1,0:T(1,128)S(1)} %bitcast.21, f32[8,8192]{1,0:T(8,128)S(1)} %copy-done.2), custom_call_target="tpu_custom_call" | custom-call | flops 536870912 | bytes 327680 | tf_op jit(solution)/shard_map/pallas_call | solution.py:202
  20.0 0.0 copy-start.5
  20.0 0.1 reshape.100
  20.1 0.1 reshape.101.from_ref
  20.2 0.0 copy-done.9
  20.2 0.1 reduce.index_ref
  20.3 1.1 shard_map.114.send_ref
  21.4 9.1 %shard_map.115.from_ref = f32[32,4,128]{2,1,0:T(4,128)S(1)} custom-call(f32[32,4,128]{2,1,0:T(4,128)S(1)} %shard_map.114.send_ref), custom_call_target="tpu_custom_call" | custom-call | tf_op jit(solution)/shard_map/pallas_call | solution.py:148
  30.5 0.0 copy-done.6
  30.5 0.1 copy.21
  30.5 0.0 copy-done.7
  30.5 0.1 copy.22
  30.6 0.0 copy-done.8
  30.6 0.1 copy.23
  30.7 0.0 copy-done.5
  30.7 0.5 copy.15
  31.2 0.6 reshape.93
  31.8 0.1 pad_maximum_fusion.from_ref
  31.9 5.1 %shard_map.112 = f32[32,192,128]{2,1,0:T(8,128)S(1)} custom-call(s32[32]{0:T(128)S(1)} %reduce.index_ref, f32[16,192,128]{2,1,0:T(8,128)S(1)} %pad_maximum_fusion.from_ref), custom_call_target="tpu_custom_call" | custom-call | tf_op jit(solution)/shard_map/pallas_call | solution.py:241
  37.0 0.0 copy-start
  37.0 1.6 %copy-done = f32[32,192,128]{2,1,0:T(8,128)} copy-done((f32[32,192,128]{2,1,0:T(8,128)}, f32[32,192,128]{2,1,0:T(8,128)S(1)}, u32[]{:S(2)}) %copy-start) | copy-done | bytes 3145752
  38.6 0.0 copy-start.10
  38.6 5.2 %all-to-all-start = ((f32[32,192,128]{2,1,0:T(8,128)}), f32[32,192,128]{2,1,0:T(8,128)S(1)}, u32[]{:S(2)}, u32[]{:S(2)}) async-start(f32[32,192,128]{2,1,0:T(8,128)} %copy-done), calls=%async_computation | async-start | bytes 6291456 | tf_op jit(solution)/shard_map/all_to_all | solution.py:519
  43.8 0.0 copy-done.10
  43.8 0.8 shard_map.116
  44.6 0.1 copy.17
  44.8 1.1 reshape.102
  45.9 2.1 %copy.19 = f32[8,1,4,2,4,8,4]{0,6,5,4,3,2,1:T(4,128)} copy(f32[8,1,4,2,4,8,4]{5,3,6,4,2,0,1:T(2,128)} %bitcast.22) | data formatting | bytes 65536 | tf_op jit(solution)/shard_map/transpose | solution.py:524
  48.0 1.9 %copy.20 = f32[8,4,8,32]{3,2,1,0:T(8,128)} copy(f32[8,4,8,32]{0,3,2,1:T(8,128)} %bitcast.24) | data formatting | bytes 65536
  49.9 1.3 fusion
  51.2 0.3 copy.18
  51.5 0.1 reshape.107.mix_ref
  51.6 63.7 %all-to-all-done.recv_ref = f32[32,192,128]{2,1,0:T(8,128)S(1)} async-done(((f32[32,192,128]{2,1,0:T(8,128)}), f32[32,192,128]{2,1,0:T(8,128)S(1)}, u32[]{:S(2)}, u32[]{:S(2)}) %all-to-all-start) | async-done | bytes 3145760 | tf_op jit(solution)/shard_map/all_to_all | solution.py:519
  115.2 5.4 %shard_map.117 = (f32[5,16,32,128]{3,2,1,0:T(8,128)S(1)}, f32[16,32,128]{2,1,0:T(8,128)}) custom-call(s32[16]{0:T(128)S(1)} %and_select_fusion.index_ref.slot_ref, f32[32,192,128]{2,1,0:T(8,128)S(1)} %all-to-all-done.recv_ref, f32[32,32]{1,0:T(8,128)S(1)} %reshape.107.mix_ref), custom_call_target="tpu_custom_call" | custom-call | tf_op jit(solution)/shard_map/pallas_call | solution.py:295
  120.6 0.0 copy-start.1
  120.6 0.9 copy-done.1
  121.6 16.4 %shard_map.118 = (f32[3,16,32,128]{3,2,1,0:T(8,128)S(1)}, f32[16,32,128]{2,1,0:T(8,128)S(1)}) custom-call(f32[5,16,32,128]{3,2,1,0:T(8,128)S(1)} %get-tuple-element.12.state_ref, f32[16,32,128]{2,1,0:T(8,128)S(1)} %copy-done.1), custom_call_target="tpu_custom_call" | custom-call | tf_op jit(solution)/shard_map/pallas_call | solution.py:460
  137.9 0.9 copy.28
  138.8 0.7 copy.29
  (2 shorter events, 0.0 us)
Async XLA Ops:
  11.6 1.0 copy-start.2
  12.5 0.8 copy-start.3
  13.3 0.8 copy-start.4
  14.0 6.2 %copy-start.9 = (s32[32,1]{1,0:T(8,128)S(1)}, s32[32,1]{1,0:T(8,128)}, u32[]{:S(2)}) copy-start(s32[32,1]{1,0:T(8,128)} %shard_map.111) | copy-start | bytes 388
  14.0 16.4 %copy-start.6 = (f32[16,4096]{1,0:T(8,128)S(1)}, f32[16,4096]{1,0:T(8,128)}, u32[]{:S(2)}) copy-start(f32[16,4096]{1,0:T(8,128)} %param.9) | copy-start | bytes 786436
  14.0 16.5 %copy-start.7 = (f32[16,4096]{1,0:T(8,128)S(1)}, f32[16,4096]{1,0:T(8,128)}, u32[]{:S(2)}) copy-start(f32[16,4096]{1,0:T(8,128)} %param.10) | copy-start | bytes 786436
  14.0 16.6 %copy-start.8 = (f32[16,4096]{1,0:T(8,128)S(1)}, f32[16,4096]{1,0:T(8,128)}, u32[]{:S(2)}) copy-start(f32[16,4096]{1,0:T(8,128)} %param.11) | copy-start | bytes 786436
  20.0 10.7 %copy-start.5 = (f32[16,3,4096]{2,0,1:T(8,128)S(1)}, f32[16,3,4096]{2,0,1:T(8,128)}, u32[]{:S(2)}) copy-start(f32[16,3,4096]{2,0,1:T(8,128)} %param.8) | copy-start | bytes 2359300
  37.0 1.6 %copy-start = (f32[32,192,128]{2,1,0:T(8,128)}, f32[32,192,128]{2,1,0:T(8,128)S(1)}, u32[]{:S(2)}) copy-start(f32[32,192,128]{2,1,0:T(8,128)S(1)} %shard_map.112) | copy-start | bytes 9437188
  38.6 5.2 %copy-start.10 = (s32[16]{0:T(128)S(1)}, s32[16]{0:T(128)}, u32[]{:S(2)}) copy-start(s32[16]{0:T(128)} %param.15) | copy-start | bytes 196
  38.6 76.6 %all-to-all-start = ((f32[32,192,128]{2,1,0:T(8,128)}), f32[32,192,128]{2,1,0:T(8,128)S(1)}, u32[]{:S(2)}, u32[]{:S(2)}) async-start(f32[32,192,128]{2,1,0:T(8,128)} %copy-done), calls=%async_computation | async-start | bytes 6291456 | tf_op jit(solution)/shard_map/all_to_all | solution.py:519
  120.6 1.0 copy-start.1
